TPU v7x, 32 devices: a whole 2x2x4 slice. The times are simulated.
32 devices in a mesh: subj: 4 (over x, core), blk: 8 (over z, y).
Axes of the slice: x: 2, y: 2, z: 4, core: 2. Of those that a mesh axis runs over, the one named last changes fastest.
Arguments:
- series: bfloat16 [8, 1200, 8192], P('subj', None, 'blk'), may hold values from -170 to 170
- circle_step: int32 [1], replicated, may hold values from 1 to 7
- vertex_count: int32 [8], replicated, may hold values from 1 to 1024, 7168 in all
Outputs:
- group_z: float32 [1024, 8192], P('subj', 'blk')
Inputs may be any that keep to these rules, and one draw needn't show every extreme that they name: `vertex_count`: the counts sum to 7168.
All inputs are finite; a program needn't handle non-finite values.
Results may differ from a plain program's by a relative error of at most 0.0019.
Values may be sent and summed in bfloat16 or wider, within the bound.
A program may use at most 192 MiB of HBM per device.

v0:
```python
import math

import jax
import jax.numpy as jnp
from jax import lax
from jax.sharding import PartitionSpec as P

tr_seconds = 0.72
low_cut = 0.01
high_cut = 0.08
shrink = 0.98
epsilon = 1e-06


def shifted(value, axis, steps):
    count = lax.axis_size(axis)
    pairs = [(source, (source + steps) % count) for source in range(count)]
    return lax.ppermute(value, axis, pairs)


def tables(frames):
    index_row = jnp.arange(frames, dtype=jnp.int32)
    product_index = (2 * index_row[None, :] + 1) * index_row[:, None] % (4 * frames)
    phase_angle = product_index.astype(jnp.float32) * (math.pi / (2 * frames))
    row_scale = jnp.where(index_row == 0, math.sqrt(0.5), 1.0).astype(jnp.float32)
    cosine_table = jnp.cos(phase_angle) * math.sqrt(2.0 / frames) * row_scale[:, None]
    frequency = index_row.astype(jnp.float32) / (2 * frames * tr_seconds)
    high_pass = frequency / low_cut / jnp.sqrt(1.0 + (frequency / low_cut) ** 2)
    low_pass = 1.0 / jnp.sqrt(1.0 + (frequency / high_cut) ** 2)
    return (cosine_table.astype(jnp.bfloat16), (high_pass * low_pass)[:, None])


def normalize(raw_block, cosine_table, gains):
    coefficients = jnp.dot(cosine_table, raw_block, preferred_element_type=jnp.float32)
    weighted = (coefficients * gains).astype(jnp.bfloat16)
    filtered = jnp.dot(cosine_table.T, weighted, preferred_element_type=jnp.float32)
    frame_mean = jnp.mean(filtered, axis=0, keepdims=True)
    centered = filtered - frame_mean
    variance = jnp.mean(centered * centered, axis=0, keepdims=True)
    return (centered * lax.rsqrt(variance + epsilon)).astype(jnp.bfloat16)


def normalize_all(series, cosine_table, gains):
    return jnp.stack(
        [normalize(series[subject], cosine_table, gains) for subject in range(series.shape[0])]
    )


def fisher(correlation):
    scaled = shrink * correlation
    return 0.5 * (jnp.log(1.0 + scaled) - jnp.log(1.0 - scaled))


def local(series, circle_step, vertex_count):
    subj_local, frames, width = series.shape
    cosine_table, gains = tables(frames)
    shift_count = circle_step[0]
    block_total = lax.axis_size("blk")
    own_block = lax.axis_index("blk")
    partner = (own_block - shift_count) % block_total
    bit_count = (block_total - 1).bit_length()
    own_z = normalize_all(series, cosine_table, gains)
    payload = own_z
    for bit_pos in range(bit_count):
        moved = shifted(payload, "blk", 1 << bit_pos)
        use_moved = shift_count >> bit_pos & 1 == 1
        payload = jnp.where(use_moved, moved, payload)
    subj_total = lax.axis_size("subj")
    subj_index = lax.axis_index("subj")
    row_share = width // subj_total
    running = jnp.zeros((row_share * lax.axis_size("subj"), width), jnp.float32)
    for subject in range(subj_local):
        slice_rows = payload[subject]
        correlation = (
            lax.dot_general(
                slice_rows,
                own_z[subject],
                (((0,), (0,)), ((), ())),
                preferred_element_type=jnp.float32,
            )
            / frames
        )
        running = running + fisher(correlation)
    summed = lax.psum_scatter(running, "subj", scatter_dimension=0, tiled=True)
    block_ids = jnp.arange(block_total, dtype=jnp.int32)
    own_count = jnp.sum(jnp.where(block_ids == own_block, vertex_count, 0))
    partner_count = jnp.sum(jnp.where(block_ids == partner, vertex_count, 0))
    row_slots = subj_index * row_share + jnp.arange(row_share, dtype=jnp.int32)
    col_slots = jnp.arange(width, dtype=jnp.int32)
    keep_mask = (row_slots < partner_count)[:, None] & (col_slots < own_count)[None, :]
    return jnp.where(keep_mask, summed / (subj_local * subj_total), 0.0)


def solution(mesh):
    in_specs = (P("subj", None, "blk"), P(), P())
    out_specs = P("subj", "blk")
    return jax.shard_map(local, mesh=mesh, in_specs=in_specs, out_specs=out_specs, check_vma=False)
```

profile of v0, /device:TPU:0, one launch (start us, length us, event | category | flops | bytes accessed | tf_op | source)
XLA Modules:
  0.0 656.4 jit_solution(9120654123698207600)
XLA Ops:
  6.5 0.0 reduce-scatter.2.cloned.1.call-start
  6.6 23.6 %fusion.12.clone.5 = bf16[1200,1200]{1,0:T(8,128)(2,1)S(1)} fusion(f32[1200]{0:T(1024)S(1)} %get-tuple-element.12, s32[1200]{0:T(1024)S(1)} %multiply_add_fusion), kind=kLoop, calls=%fused_computation.5.clone.2.clone.clone.clone.2 | loop fusion | flops 15840000 | bytes 2889600 | tf_op jit(solution)/shard_map/reduce_sum | solution.py:37
  30.2 24.6 %fusion.9.clone.5 = bf16[1200,1200]{1,0:T(8,128)(2,1)} fusion(f32[1200]{0:T(1024)S(1)} %get-tuple-element.12, s32[1200]{0:T(1024)S(1)} %multiply_add_fusion), kind=kLoop, calls=%fused_computation.5.clone.clone.clone.clone.2 | loop fusion | flops 15840000 | bytes 2889600 | tf_op jit(solution)/shard_map/reduce_sum | solution.py:37
  54.8 35.4 %fusion.49 = (f32[1024]{0:T(1024)S(1)}, f32[1200,1024]{1,0:T(8,128)}) fusion(f32[1200]{0:T(1024)S(1)} %get-tuple-element.12, s32[1200]{0:T(1024)S(1)} %multiply_add_fusion, f32[1200]{0:T(1024)S(1)} %get-tuple-element.11, bf16[2,1200,1024]{2,1,0:T(8,128)(2,1)} %param.3, bf16[1200,1200]{1,0:T(8,128)(2,1)S(1)} %fusion.12.clone.5), kind=kOutput, calls=%fused_computation.55 | convolution fusion | flops 5917765632 | bytes 10271296 | tf_op jit(solution)/shard_map/dot_general | solution.py:36
  90.2 3.1 multiply_reduce_fusion.1
  93.3 0.8 copy-done.1
  94.1 0.7 fusion.28
  94.8 46.3 %fusion.44 = (f32[1024]{0:T(1024)S(1)}, f32[1200,1024]{1,0:T(8,128)}) fusion(f32[1200]{0:T(1024)S(1)} %get-tuple-element.12, s32[1200]{0:T(1024)S(1)} %multiply_add_fusion, bf16[2,1200,1024]{2,1,0:T(8,128)(2,1)} %param.3, f32[1200]{0:T(1024)S(1)} %get-tuple-element.11, bf16[1200,1200]{1,0:T(8,128)(2,1)} %fusion.9.clone.5), kind=kOutput, calls=%fused_computation.54 | convolution fusion | flops 5917765632 | bytes 10463296 | tf_op jit(solution)/shard_map/dot_general | solution.py:36
  141.1 3.1 multiply_reduce_fusion
  144.2 0.7 copy-done.2
  145.0 0.8 fusion.29
  145.7 2.9 pad_maximum_fusion
  148.6 3.0 collective-permute-start
  152.2 108.7 %collective-permute-done = bf16[2,1200,1024]{2,1,0:T(8,128)(2,1)} collective-permute-done((bf16[2,1200,1024]{2,1,0:T(8,128)(2,1)}, bf16[2,1200,1024]{2,1,0:T(8,128)(2,1)}, u32[]{:S(2)}, u32[]{:S(2)}) %collective-permute-start) | collective-permute-done | bytes 4915232 | tf_op jit(solution)/shard_map/ppermute | solution.py:18
  260.9 4.5 broadcast_select_fusion
  265.5 0.0 collective-permute-start.1
  265.5 109.3 %collective-permute-done.1 = bf16[2,1200,1024]{2,1,0:T(8,128)(2,1)} collective-permute-done((bf16[2,1200,1024]{2,1,0:T(8,128)(2,1)}, bf16[2,1200,1024]{2,1,0:T(8,128)(2,1)}, u32[]{:S(2)}, u32[]{:S(2)}) %collective-permute-start.1) | collective-permute-done | bytes 4915232 | tf_op jit(solution)/shard_map/ppermute | solution.py:18
  374.8 6.2 broadcast_select_fusion.1
  381.0 0.0 collective-permute-start.2
  381.0 211.0 %collective-permute-done.2 = bf16[2,1200,1024]{2,1,0:T(8,128)(2,1)} collective-permute-done((bf16[2,1200,1024]{2,1,0:T(8,128)(2,1)}, bf16[2,1200,1024]{2,1,0:T(8,128)(2,1)}, u32[]{:S(2)}, u32[]{:S(2)}) %collective-permute-start.2) | collective-permute-done | bytes 4915232 | tf_op jit(solution)/shard_map/ppermute | solution.py:18
  592.1 3.0 broadcast_select_fusion.2
  595.0 0.0 slice-done
  595.1 0.0 slice-start.3
  595.1 3.0 fusion.15
  598.2 0.0 copy-start.3
  598.2 6.3 add_multiply_fusion
  604.5 0.0 reduce-scatter.2.cloned.1.call-update
  604.6 0.7 fusion.30
  605.3 0.7 add_compare_fusion
  606.0 0.7 iota_compare_fusion.1
  606.7 40.3 %reduce-scatter.2.cloned.1.call-done = f32[256,1024]{1,0:T(8,128)} async-done(((f32[1024,1024]{1,0:T(8,128)}), f32[256,1024]{1,0:T(8,128)}) %reduce-scatter.2.cloned.1.call-update) | async-done | bytes 1048592 | tf_op jit(solution)/shard_map/reduce_scatter | solution.py:84
  647.0 2.4 multiply_select_fusion
  (19 shorter events, 0.1 us)
Async XLA Ops:
  6.5 640.4 %reduce-scatter.2.cloned.1.call-start = ((), (), s32[]{:S(2)}) async-start(), calls=%async_computation.1 | async-start | bytes 5242880 | tf_op jit(solution)/shard_map/reduce_scatter | solution.py:84
  90.2 3.9 copy-start.1
  141.1 3.9 copy-start.2
  145.7 6.5 copy-start
  148.6 112.3 %collective-permute-start = (bf16[2,1200,1024]{2,1,0:T(8,128)(2,1)}, bf16[2,1200,1024]{2,1,0:T(8,128)(2,1)}, u32[]{:S(2)}, u32[]{:S(2)}) collective-permute-start(bf16[2,1200,1024]{2,1,0:T(8,128)(2,1)} %pad_maximum_fusion), channel_id=1, source_target_pairs={{0,1},{1,2},{2,3},{3,4},{4,5},{5,6},{6,7},{7,0},{8,9},{9,10},{10,1... | collective-permute-start | bytes 14745608 | tf_op jit(solution)/shard_map/ppermute | solution.py:18
  265.5 109.3 %collective-permute-start.1 = (bf16[2,1200,1024]{2,1,0:T(8,128)(2,1)}, bf16[2,1200,1024]{2,1,0:T(8,128)(2,1)}, u32[]{:S(2)}, u32[]{:S(2)}) collective-permute-start(bf16[2,1200,1024]{2,1,0:T(8,128)(2,1)} %broadcast_select_fusion), channel_id=1, source_target_pairs={{0,2},{1,3},{2,4},{3,5},{4,6},{5,7},{6,0},{7,1},{8,10},{9,11},{10,... | collective-permute-start | bytes 14745608 | tf_op jit(solution)/shard_map/ppermute | solution.py:18
  381.0 211.0 %collective-permute-start.2 = (bf16[2,1200,1024]{2,1,0:T(8,128)(2,1)}, bf16[2,1200,1024]{2,1,0:T(8,128)(2,1)}, u32[]{:S(2)}, u32[]{:S(2)}) collective-permute-start(bf16[2,1200,1024]{2,1,0:T(8,128)(2,1)} %broadcast_select_fusion.1), channel_id=1, source_target_pairs={{0,4},{1,5},{2,6},{3,7},{4,0},{5,1},{6,2},{7,3},{8,12},{9,13},{10,... | collective-permute-start | bytes 14745608 | tf_op jit(solution)/shard_map/ppermute | solution.py:18
  381.0 214.0 %slice-start = ((s8[4915200]{0:T(1024)(128)(4,1)}), s8[720896]{0:T(1024)(128)(4,1)S(1)}, s32[]{:S(2)}) async-start(s8[4915200]{0:T(1024)(128)(4,1)} %bitcast.39), calls=%async_computation.2 | async-start | bytes 1441792
  381.0 214.0 %slice-start.1 = ((s8[4915200]{0:T(1024)(128)(4,1)}), s8[4194304]{0:T(1024)(128)(4,1)S(1)}, s32[]{:S(2)}) async-start(s8[4915200]{0:T(1024)(128)(4,1)} %bitcast.39), calls=%async_computation.3 | async-start | bytes 8388608
  592.1 6.1 slice-start.2
  595.1 3.1 slice-start.3
  598.2 6.4 copy-start.3
Sparse Core Ops, SparseCore 0:
  604.7 42.2 reduce-scatter.1
where the time goes:
time: 655 us; the launch traced here: 656 us
  waiting for transfers between devices  469 us (72%)
  matrix products  91 us (14%)
  other arithmetic  77 us (12%)
  between operations  14.5 us (2%)
    ppermute x3, waiting for transfers between devices, shifted(): return lax.ppermute(value, axis, pairs)  429 us
    dot_general x2, matrix products, normalize(): jnp.dot(cosine_table.T, weighted, preferred_element_type=jnp.float32)  81.6 us
    reduce_sum x2, other arithmetic, normalize(): frame_mean = jnp.mean(filtered, axis=0, keepdims=True)  48.3 us
    reduce_scatter x1, waiting for transfers between devices, local(): summed = lax.psum_scatter(running, 'subj', scatter_dimension=0, tiled=True)  40.3 us
    select_n x3, other arithmetic, local(): payload = jnp.where(use_moved, moved, payload)  13.7 us
  transfers between devices with their start and end apart: 4, of which 4 were waited for; matrix products, arithmetic and copies ran while one was open for 0% of the time, Pallas kernels for 0%

commit v1 on v0

v1 whole, which is shorter than its diff:
```python
import math

import jax
import jax.numpy as jnp
import numpy as np
from jax import lax
from jax.experimental import pallas as pl
from jax.experimental.pallas import tpu as pltpu
from jax.sharding import PartitionSpec as P

tr_seconds = 0.72
low_cut = 0.01
high_cut = 0.08
shrink = 0.98
epsilon = 1e-06
tile = 256
vmem_limit = 48 * 1024 * 1024


def tables(frames):
    index_row = np.arange(frames, dtype=np.int64)
    product_index = (2 * index_row[None, :] + 1) * index_row[:, None] % (4 * frames)
    phase_angle = product_index.astype(np.float64) * (math.pi / (2 * frames))
    row_scale = np.where(index_row == 0, math.sqrt(0.5), 1.0)
    cosine_table = np.cos(phase_angle) * math.sqrt(2.0 / frames) * row_scale[:, None]
    frequency = index_row.astype(np.float64) / (2 * frames * tr_seconds)
    high_pass = frequency / low_cut / np.sqrt(1.0 + (frequency / low_cut) ** 2)
    low_pass = 1.0 / np.sqrt(1.0 + (frequency / high_cut) ** 2)
    cosine_table = cosine_table.astype(jnp.bfloat16)
    gains = (high_pass * low_pass).astype(np.float32)[:, None]
    return cosine_table, np.ascontiguousarray(cosine_table.T), gains


def normalize(raw, table, table_t, gains):
    coefficients = jnp.dot(table, raw, preferred_element_type=jnp.float32)
    weighted = (coefficients * gains).astype(jnp.bfloat16)
    filtered = jnp.dot(table_t, weighted, preferred_element_type=jnp.float32)
    frames = filtered.shape[0]
    frame_mean = jnp.sum(filtered, axis=0, keepdims=True) * (1.0 / frames)
    centered = filtered - frame_mean
    variance = jnp.sum(centered * centered, axis=0, keepdims=True) * (1.0 / frames)
    return (centered * lax.rsqrt(variance + epsilon)).astype(jnp.bfloat16)


def own_kernel(raw_ref, table_ref, table_t_ref, gains_ref, z_ref):
    z_ref[0] = normalize(raw_ref[0], table_ref[...], table_t_ref[...], gains_ref[...])


def partner_kernel(raw_ref, own_ref, table_ref, table_t_ref, gains_ref, out_ref, z_scr):
    subjects, frames, _ = raw_ref.shape
    width = own_ref.shape[2]
    for subject in range(subjects):
        z_scr[subject] = normalize(
            raw_ref[subject], table_ref[...], table_t_ref[...], gains_ref[...]
        ).T
    for col in range(0, width, tile):
        above = None
        below = None
        for subject in range(subjects):
            correlation = jnp.dot(
                z_scr[subject],
                own_ref[subject, :, col : col + tile],
                preferred_element_type=jnp.float32,
            )
            scaled = correlation * (shrink / frames)
            above = 1.0 + scaled if above is None else above * (1.0 + scaled)
            below = 1.0 - scaled if below is None else below * (1.0 - scaled)
        out_ref[:, col : col + tile] = 0.5 * jnp.log(above / below)


def normalize_own(series, table, table_t, gains):
    subjects, frames, width = series.shape
    whole = lambda array: pl.BlockSpec(array.shape, lambda s, c: (0, 0))
    block = pl.BlockSpec((1, frames, tile), lambda s, c: (s, 0, c))
    return pl.pallas_call(
        own_kernel,
        grid=(subjects, width // tile),
        in_specs=[block, whole(table), whole(table_t), whole(gains)],
        out_specs=block,
        out_shape=jax.ShapeDtypeStruct(series.shape, jnp.bfloat16),
        compiler_params=pltpu.CompilerParams(vmem_limit_bytes=vmem_limit),
        cost_estimate=pl.CostEstimate(
            flops=4 * subjects * frames * frames * width,
            bytes_accessed=4 * series.size + 4 * frames * frames,
            transcendentals=0,
        ),
    )(series, table, table_t, gains)


def partner_rows(raw, own_z, table, table_t, gains):
    subjects, frames, rows = raw.shape
    width = own_z.shape[2]
    return pl.pallas_call(
        partner_kernel,
        in_specs=[pl.BlockSpec(memory_space=pltpu.VMEM)] * 5,
        out_specs=pl.BlockSpec(memory_space=pltpu.VMEM),
        out_shape=jax.ShapeDtypeStruct((rows, width), jnp.float32),
        scratch_shapes=[pltpu.VMEM((subjects, rows, frames), jnp.bfloat16)],
        compiler_params=pltpu.CompilerParams(vmem_limit_bytes=vmem_limit),
        cost_estimate=pl.CostEstimate(
            flops=subjects * rows * frames * (4 * frames + 2 * width),
            bytes_accessed=2 * raw.size + 2 * own_z.size + 4 * frames * frames + 4 * rows * width,
            transcendentals=rows * width,
        ),
    )(raw, own_z, table, table_t, gains)


def tile_rows(step, block_total, series, constants):
    pairs = [(source, (source + step) % block_total) for source in range(block_total)]
    width = series.shape[2]
    share = width // lax.axis_size("subj")
    chunks = [
        lax.ppermute(series[:, :, start : start + share], "blk", pairs)
        for start in range(0, width, share)
    ]
    own_z = normalize_own(series, *constants)
    core = lax.axis_index("subj") % 2
    core_pairs = [(0, 1), (1, 0), (2, 3), (3, 2)]
    sums = []
    for half in range(2):
        even, odd = (
            partner_rows(chunks[2 * half + part], own_z, *constants) for part in range(2)
        )
        kept = jnp.where(core == 0, even, odd)
        given = jnp.where(core == 0, odd, even)
        sums.append(kept + lax.ppermute(given, "subj", core_pairs))
    return sums


def local(series, circle_step, vertex_count):
    subj_local, frames, width = series.shape
    constants = [jnp.asarray(table) for table in tables(frames)]
    block_total = lax.axis_size("blk")
    subj_total = lax.axis_size("subj")
    subj_index = lax.axis_index("subj")
    own_block = lax.axis_index("blk")
    partner = (own_block - circle_step[0]) % block_total

    def branch(step):
        return lambda raw: tile_rows(step, block_total, raw, constants)

    low, high = lax.switch(
        circle_step[0] - 1, [branch(step) for step in range(1, block_total)], series
    )
    on_low = subj_index < 2
    given = jnp.where(on_low, high, low).astype(jnp.bfloat16)
    kept = jnp.where(on_low, low, high)
    taken = lax.ppermute(given, "subj", [(0, 2), (1, 3), (2, 0), (3, 1)])
    summed = kept + taken.astype(jnp.float32)
    row_share = width // subj_total
    block_ids = jnp.arange(block_total, dtype=jnp.int32)
    own_count = jnp.sum(jnp.where(block_ids == own_block, vertex_count, 0))
    partner_count = jnp.sum(jnp.where(block_ids == partner, vertex_count, 0))
    row_slots = subj_index * row_share + jnp.arange(row_share, dtype=jnp.int32)
    col_slots = jnp.arange(width, dtype=jnp.int32)
    keep_mask = (row_slots < partner_count)[:, None] & (col_slots < own_count)[None, :]
    return jnp.where(keep_mask, summed / (subj_local * subj_total), 0.0)


def solution(mesh):
    in_specs = (P("subj", None, "blk"), P(), P())
    out_specs = P("subj", "blk")
    return jax.shard_map(local, mesh=mesh, in_specs=in_specs, out_specs=out_specs, check_vma=False)
```

time: 655 us -> 173 us (0.26)
  waiting for transfers between devices: 469 us -> 52 us
  matrix products: 91 us -> 0 us
  Pallas kernels: 0 us -> 72 us
  other arithmetic: 77 us -> 6.4 us
  loops' own time: 0 us -> 26.6 us
  between operations: 14.5 us -> 0.97 us
    ppermute x3 -> x7, waiting for transfers between devices: 429 us -> 52 us  [the longest x4 38 us: tile_rows(): lax.ppermute(series[:, :, start:start + share], 'blk', pairs)]
    dot_general x4 -> x0, matrix products: 91 us -> none  [the longest x2 81.6 us: normalize(): jnp.dot(cosine_table.T, weighted, preferred_element_type=jnp.float32)]
    pallas_call x0 -> x5, Pallas kernels: none -> 72 us  [the longest x4 40.2 us: partner_rows(): pl.pallas_call(partner_kernel, in_specs=[pl.BlockSpec(memory_space=pltpu....]
    reduce_sum x4 -> x0, other arithmetic: 54.5 us -> none  [the longest x2 48.3 us: normalize(): frame_mean = jnp.mean(filtered, axis=0, keepdims=True)]
    reduce_scatter x1 -> x0, waiting for transfers between devices: 40.3 us -> none  [local(): summed = lax.psum_scatter(running, 'subj', scatter_dimension=0, tiled=True)]
    another operation x0 -> x1, loops' own time: none -> 26.6 us  [local(): lax.switch(circle_step[0] - 1, [branch(step) for step in range(1, block_t...]
    select_n x3 -> x2, other arithmetic: 13.7 us -> 0.32 us  [tile_rows(): given = jnp.where(core == 0, odd, even)]
  transfers between devices with their start and end apart: 4 -> 7, of which waited for: 4 -> 5; matrix products, arithmetic and copies ran while one was open for 0% -> 1% of each run, Pallas kernels for 0% -> 41%
where the time goes in v1:
time: 173 us; the launch traced here: 174 us
  Pallas kernels  72 us (42%)
  waiting for transfers between devices  52 us (30%)
  loops' own time  26.6 us (15%)
  starting transfers between devices  8.9 us (5%)
  local copies, waits for them, and re-layouts  7.45 us (4%)
  other arithmetic  6.4 us (4%)
    pallas_call x4, Pallas kernels, partner_rows(): pl.pallas_call(partner_kernel, in_specs=[pl.BlockSpec(memory_space=pltpu....  40.2 us
    ppermute x4, waiting for transfers between devices, tile_rows(): lax.ppermute(series[:, :, start:start + share], 'blk', pairs)  38 us
    pallas_call x1, Pallas kernels, normalize_own(): pl.pallas_call(own_kernel, grid=(subjects, width // tile), in_specs=[bloc...  31.8 us
    another operation x1, loops' own time, local(): lax.switch(circle_step[0] - 1, [branch(step) for step in range(1, block_t...  26.6 us
    ppermute x1, waiting for transfers between devices, local(): taken = lax.ppermute(given, 'subj', [(0, 2), (1, 3), (2, 0), (3, 1)])  11.7 us
    ppermute x4, starting transfers between devices, tile_rows(): lax.ppermute(series[:, :, start:start + share], 'blk', pairs)  8.42 us
    slice x1, local copies, waits for them, and re-layouts, tile_rows(): series[:, :, start:start + share]  5.18 us
  transfers between devices with their start and end apart: 7, of which 5 were waited for; matrix products, arithmetic and copies ran while one was open for 1% of the time, Pallas kernels for 41%

profile of v1, /device:TPU:0, one launch (start us, length us, event | category | flops | bytes accessed | tf_op | source)
XLA Modules:
  0.0 174.4 jit_solution(12597338677244156654)
XLA Ops:
  0.7 156.8 %conditional.1 = (f32[256,1024]{1,0:T(8,128)S(1)}, f32[256,1024]{1,0:T(8,128)}) conditional(s32[]{:T(128)} %clamp.3, (bf16[2,1200,1024]{2,1,0:T(8,128)(2,1)}, bf16[1200,1200]{1,0:T(8,128)(2,1)}, bf16[1200,1200]{1,0:T(8,128)(2,1)}, f32[1200,1]{1,0:T(8,128)}) %tuple.33, (bf16[2,1200,1024]{2,1,0:T(8,128)(2,1)}, ...), branch_computations={%region_2.3_spmd, %region_3.4_spmd, %region_4.5_spmd, %region_5.6_... | conditional | flops 28627697664 | bytes 193881200 | solution.py:142
  26.9 0.0 copy-start.27
  27.0 0.0 copy-start.48
  27.0 5.2 %fusion.8 = (bf16[2,1200,256]{2,1,0:T(8,128)(2,1)}, bf16[2,1200,256]{2,1,0:T(8,128)(2,1)}, bf16[2,1200,256]{2,1,0:T(8,128)(2,1)}, bf16[2,1200,256]{2,1,0:T(8,128)(2,1)}) fusion(bf16[2,1200,1024]{2,1,0:T(8,128)(2,1)} %get-tuple-element.85.raw_ref), kind=kLoop, calls=%fused_computation.42 | loop fusion | bytes 9830400 | tf_op jit(solution)/shard_map/cond/branch_6_fun/slice | solution.py:113
  32.2 6.0 %collective-permute-start.37 = (bf16[2,1200,256]{2,1,0:T(8,128)(2,1)}, bf16[2,1200,256]{2,1,0:T(8,128)(2,1)}, u32[]{:S(2)}, u32[]{:S(2)}) collective-permute-start(bf16[2,1200,256]{2,1,0:T(8,128)(2,1)} %get-tuple-element.121), channel_id=1, source_target_pairs={{0,7},{1,0},{2,1},{3,2},{4,3},{5,4},{6,5},{7,6},{8,15},{9,8},{10,9... | collective-permute-start | bytes 3686408 | tf_op jit(solution)/shard_map/cond/branch_6_fun/ppermute | solution.py:113
  38.2 0.5 collective-permute-start.36
  38.7 1.4 collective-permute-start.40
  40.1 0.5 collective-permute-start.39
  40.6 31.8 %branch_6_fun.5.own_ref = bf16[2,1200,1024]{2,1,0:T(8,128)(2,1)S(1)} custom-call(bf16[2,1200,1024]{2,1,0:T(8,128)(2,1)S(1)} %copy-done.13, bf16[1200,1200]{1,0:T(8,128)(2,1)S(1)} %copy-done.27, bf16[1200,1200]{1,0:T(8,128)(2,1)} %get-tuple-element.87.table_t_ref, f32[1200,1]{1,0:T(8,128)S(1)} %copy-done.48), custom_call_target="tpu_custom_call" | custom-call | flops 11796480000 | bytes 15590400 | tf_op jit(solution)/shard_map/cond/branch_6_fun/pallas_call | solution.py:75
  72.4 2.2 %copy-done.6 = bf16[2,1200,1024]{2,1,0:T(8,128)(2,1)} copy-done((bf16[2,1200,1024]{2,1,0:T(8,128)(2,1)}, bf16[2,1200,1024]{2,1,0:T(8,128)(2,1)S(1)}, u32[]{:S(2)}) %copy-start.6) | copy-done | bytes 4915224 | tf_op jit(solution)/shard_map/cond
  74.6 11.6 %branch_6_fun.7 = f32[256,1024]{1,0:T(8,128)S(1)} custom-call(bf16[2,1200,256]{2,1,0:T(8,128)(2,1)} %collective-permute-done.37.raw_ref, bf16[2,1200,1024]{2,1,0:T(8,128)(2,1)} %copy-done.6, bf16[1200,1200]{1,0:T(8,128)(2,1)} %get-tuple-element.86.table_ref, bf16[1200,1200]{1,0:T(8,128)(2,1)} %get-tuple-element.87.table_t_ref, f32[1200,1]{1,0:T(8,128)S(1)} %copy-done.48), custom_call_target="tpu_custom_call" | custom-call | flops 4207411200 | bytes 12952576 | tf_op jit(solution)/shard_map/cond/branch_6_fun/pallas_call | solution.py:93
  86.2 6.0 %collective-permute-done.36.raw_ref = bf16[2,1200,256]{2,1,0:T(8,128)(2,1)} collective-permute-done((bf16[2,1200,256]{2,1,0:T(8,128)(2,1)}, bf16[2,1200,256]{2,1,0:T(8,128)(2,1)}, u32[]{:S(2)}, u32[]{:S(2)}) %collective-permute-start.36) | collective-permute-done | bytes 1228832 | tf_op jit(solution)/shard_map/cond/branch_6_fun/ppermute | solution.py:113
  92.2 9.7 %branch_6_fun.6 = f32[256,1024]{1,0:T(8,128)S(1)} custom-call(bf16[2,1200,256]{2,1,0:T(8,128)(2,1)} %collective-permute-done.36.raw_ref, bf16[2,1200,1024]{2,1,0:T(8,128)(2,1)} %copy-done.6, bf16[1200,1200]{1,0:T(8,128)(2,1)S(1)} %copy-done.28, bf16[1200,1200]{1,0:T(8,128)(2,1)S(1)} %copy-done.35, f32[1200,1]{1,0:T(8,128)S(1)} %copy-done.48), custom_call_target="tpu_custom_call" | custom-call | flops 4207411200 | bytes 12952576 | tf_op jit(solution)/shard_map/cond/branch_6_fun/pallas_call | solution.py:93
  102.0 0.0 copy-start.49
  102.0 0.2 broadcast_select_fusion.13
  102.2 0.1 collective-permute-start.38
  102.3 16.3 %collective-permute-done.40.raw_ref = bf16[2,1200,256]{2,1,0:T(8,128)(2,1)S(1)} collective-permute-done((bf16[2,1200,256]{2,1,0:T(8,128)(2,1)}, bf16[2,1200,256]{2,1,0:T(8,128)(2,1)S(1)}, u32[]{:S(2)}, u32[]{:S(2)}) %collective-permute-start.40) | collective-permute-done | bytes 1228832 | tf_op jit(solution)/shard_map/cond/branch_6_fun/ppermute | solution.py:113
  118.6 9.5 %branch_6_fun.9 = f32[256,1024]{1,0:T(8,128)S(1)} custom-call(bf16[2,1200,256]{2,1,0:T(8,128)(2,1)S(1)} %collective-permute-done.40.raw_ref, bf16[2,1200,1024]{2,1,0:T(8,128)(2,1)} %copy-done.6, bf16[1200,1200]{1,0:T(8,128)(2,1)S(1)} %copy-done.28, bf16[1200,1200]{1,0:T(8,128)(2,1)S(1)} %copy-done.35, f32[1200,1]{1,0:T(8,128)S(1)} %copy-done.49), custom_call_target="tpu_custom_call" | custom-call | flops 4207411200 | bytes 12952576 | tf_op jit(solution)/shard_map/cond/branch_6_fun/pallas_call | solution.py:93
  128.1 15.6 %collective-permute-done.39.raw_ref = bf16[2,1200,256]{2,1,0:T(8,128)(2,1)S(1)} collective-permute-done((bf16[2,1200,256]{2,1,0:T(8,128)(2,1)}, bf16[2,1200,256]{2,1,0:T(8,128)(2,1)S(1)}, u32[]{:S(2)}, u32[]{:S(2)}) %collective-permute-start.39) | collective-permute-done | bytes 1228832 | tf_op jit(solution)/shard_map/cond/branch_6_fun/ppermute | solution.py:113
  143.8 9.3 %branch_6_fun.8 = f32[256,1024]{1,0:T(8,128)S(1)} custom-call(bf16[2,1200,256]{2,1,0:T(8,128)(2,1)S(1)} %collective-permute-done.39.raw_ref, bf16[2,1200,1024]{2,1,0:T(8,128)(2,1)} %copy-done.6, bf16[1200,1200]{1,0:T(8,128)(2,1)S(1)} %copy-done.28, bf16[1200,1200]{1,0:T(8,128)(2,1)S(1)} %copy-done.35, f32[1200,1]{1,0:T(8,128)S(1)} %copy-done.49), custom_call_target="tpu_custom_call" | custom-call | flops 4207411200 | bytes 12952576 | tf_op jit(solution)/shard_map/cond/branch_6_fun/pallas_call | solution.py:93
  153.1 0.1 broadcast_select_fusion.12
  153.2 0.1 collective-permute-start.41
  153.3 0.3 select_add_fusion.13
  153.6 2.4 %collective-permute-done.41 = f32[256,1024]{1,0:T(8,128)S(1)} collective-permute-done((f32[256,1024]{1,0:T(8,128)S(1)}, f32[256,1024]{1,0:T(8,128)S(1)}, u32[]{:S(2)}, u32[]{:S(2)}) %collective-permute-start.41) | collective-permute-done | bytes 1048608 | tf_op jit(solution)/shard_map/cond/branch_6_fun/ppermute | solution.py:126
  156.0 1.2 select_add_fusion.12
  157.5 1.4 select_convert_fusion
  158.8 0.3 collective-permute-start.42
  159.2 0.7 fusion
  159.9 0.6 add_compare_fusion
  160.5 0.6 iota_compare_fusion
  161.2 11.7 %collective-permute-done.42 = bf16[256,1024]{1,0:T(8,128)(2,1)S(1)} collective-permute-done((bf16[256,1024]{1,0:T(8,128)(2,1)S(1)}, bf16[256,1024]{1,0:T(8,128)(2,1)S(1)}, u32[]{:S(2)}, u32[]{:S(2)}) %collective-permute-start.42) | collective-permute-done | bytes 524320 | tf_op jit(solution)/shard_map/ppermute | solution.py:148
  172.9 1.2 multiply_select_fusion
  (14 shorter events, 0.0 us)
Async XLA Ops:
  26.9 13.6 %copy-start.13 = (bf16[2,1200,1024]{2,1,0:T(8,128)(2,1)S(1)}, bf16[2,1200,1024]{2,1,0:T(8,128)(2,1)}, u32[]{:S(2)}) copy-start(bf16[2,1200,1024]{2,1,0:T(8,128)(2,1)} %get-tuple-element.85.raw_ref) | copy-start | bytes 14745604 | tf_op jit(solution)/shard_map/cond
  26.9 13.6 %copy-start.27 = (bf16[1200,1200]{1,0:T(8,128)(2,1)S(1)}, bf16[1200,1200]{1,0:T(8,128)(2,1)}, u32[]{:S(2)}) copy-start(bf16[1200,1200]{1,0:T(8,128)(2,1)} %get-tuple-element.86.table_ref) | copy-start | bytes 8640004 | tf_op jit(solution)/shard_map/cond
  27.0 13.6 %copy-start.48 = (f32[1200,1]{1,0:T(8,128)S(1)}, f32[1200,1]{1,0:T(8,128)}, u32[]{:S(2)}) copy-start(f32[1200,1]{1,0:T(8,128)} %get-tuple-element.88.gains_ref) | copy-start | bytes 14404 | tf_op jit(solution)/shard_map/cond
  32.2 42.5 %collective-permute-start.37 = (bf16[2,1200,256]{2,1,0:T(8,128)(2,1)}, bf16[2,1200,256]{2,1,0:T(8,128)(2,1)}, u32[]{:S(2)}, u32[]{:S(2)}) collective-permute-start(bf16[2,1200,256]{2,1,0:T(8,128)(2,1)} %get-tuple-element.121), channel_id=1, source_target_pairs={{0,7},{1,0},{2,1},{3,2},{4,3},{5,4},{6,5},{7,6},{8,15},{9,8},{10,9... | collective-permute-start | bytes 3686408 | tf_op jit(solution)/shard_map/cond/branch_6_fun/ppermute | solution.py:113
  38.2 54.1 %collective-permute-start.36 = (bf16[2,1200,256]{2,1,0:T(8,128)(2,1)}, bf16[2,1200,256]{2,1,0:T(8,128)(2,1)}, u32[]{:S(2)}, u32[]{:S(2)}) collective-permute-start(bf16[2,1200,256]{2,1,0:T(8,128)(2,1)} %get-tuple-element.122), channel_id=1, source_target_pairs={{0,7},{1,0},{2,1},{3,2},{4,3},{5,4},{6,5},{7,6},{8,15},{9,8},{10,9... | collective-permute-start | bytes 3686408 | tf_op jit(solution)/shard_map/cond/branch_6_fun/ppermute | solution.py:113
  38.7 79.9 %collective-permute-start.40 = (bf16[2,1200,256]{2,1,0:T(8,128)(2,1)}, bf16[2,1200,256]{2,1,0:T(8,128)(2,1)S(1)}, u32[]{:S(2)}, u32[]{:S(2)}) collective-permute-start(bf16[2,1200,256]{2,1,0:T(8,128)(2,1)} %get-tuple-element.120), channel_id=1, source_target_pairs={{0,7},{1,0},{2,1},{3,2},{4,3},{5,4},{6,5},{7,6},{8,15},{9,8},{10,9... | collective-permute-start | bytes 3686408 | tf_op jit(solution)/shard_map/cond/branch_6_fun/ppermute | solution.py:113
  40.1 103.7 %collective-permute-start.39 = (bf16[2,1200,256]{2,1,0:T(8,128)(2,1)}, bf16[2,1200,256]{2,1,0:T(8,128)(2,1)S(1)}, u32[]{:S(2)}, u32[]{:S(2)}) collective-permute-start(bf16[2,1200,256]{2,1,0:T(8,128)(2,1)} %get-tuple-element.119), channel_id=1, source_target_pairs={{0,7},{1,0},{2,1},{3,2},{4,3},{5,4},{6,5},{7,6},{8,15},{9,8},{10,9... | collective-permute-start | bytes 3686408 | tf_op jit(solution)/shard_map/cond/branch_6_fun/ppermute | solution.py:113
  72.4 2.2 %copy-start.6 = (bf16[2,1200,1024]{2,1,0:T(8,128)(2,1)}, bf16[2,1200,1024]{2,1,0:T(8,128)(2,1)S(1)}, u32[]{:S(2)}) copy-start(bf16[2,1200,1024]{2,1,0:T(8,128)(2,1)S(1)} %branch_6_fun.5.own_ref) | copy-start | bytes 14745604 | tf_op jit(solution)/shard_map/cond
  74.6 17.6 %copy-start.28 = (bf16[1200,1200]{1,0:T(8,128)(2,1)S(1)}, bf16[1200,1200]{1,0:T(8,128)(2,1)}, u32[]{:S(2)}) copy-start(bf16[1200,1200]{1,0:T(8,128)(2,1)} %get-tuple-element.86.table_ref) | copy-start | bytes 8640004 | tf_op jit(solution)/shard_map/cond
  74.6 17.6 %copy-start.35 = (bf16[1200,1200]{1,0:T(8,128)(2,1)S(1)}, bf16[1200,1200]{1,0:T(8,128)(2,1)}, u32[]{:S(2)}) copy-start(bf16[1200,1200]{1,0:T(8,128)(2,1)} %get-tuple-element.87.table_t_ref) | copy-start | bytes 8640004 | tf_op jit(solution)/shard_map/cond
  102.0 16.6 %copy-start.49 = (f32[1200,1]{1,0:T(8,128)S(1)}, f32[1200,1]{1,0:T(8,128)}, u32[]{:S(2)}) copy-start(f32[1200,1]{1,0:T(8,128)} %get-tuple-element.88.gains_ref) | copy-start | bytes 14404 | tf_op jit(solution)/shard_map/cond
  102.2 51.1 %collective-permute-start.38 = (f32[256,1024]{1,0:T(8,128)S(1)}, f32[256,1024]{1,0:T(8,128)S(1)}, u32[]{:S(2)}, u32[]{:S(2)}) collective-permute-start(f32[256,1024]{1,0:T(8,128)S(1)} %broadcast_select_fusion.13), channel_id=1, source_target_pairs={{0,8},{8,0},{16,24},{24,16},{1,9},{9,1},{17,25},{25,17},{2,10},{10... | collective-permute-start | bytes 3145736 | tf_op jit(solution)/shard_map/cond/branch_6_fun/ppermute | solution.py:126
  153.2 2.7 %collective-permute-start.41 = (f32[256,1024]{1,0:T(8,128)S(1)}, f32[256,1024]{1,0:T(8,128)S(1)}, u32[]{:S(2)}, u32[]{:S(2)}) collective-permute-start(f32[256,1024]{1,0:T(8,128)S(1)} %broadcast_select_fusion.12), channel_id=1, source_target_pairs={{0,8},{8,0},{16,24},{24,16},{1,9},{9,1},{17,25},{25,17},{2,10},{10... | collective-permute-start | bytes 3145736 | tf_op jit(solution)/shard_map/cond/branch_6_fun/ppermute | solution.py:126
  157.5 1.7 copy-start.14
  158.8 14.0 %collective-permute-start.42 = (bf16[256,1024]{1,0:T(8,128)(2,1)S(1)}, bf16[256,1024]{1,0:T(8,128)(2,1)S(1)}, u32[]{:S(2)}, u32[]{:S(2)}) collective-permute-start(bf16[256,1024]{1,0:T(8,128)(2,1)S(1)} %select_convert_fusion), channel_id=1, source_target_pairs={{0,16},{8,24},{16,0},{24,8},{1,17},{9,25},{17,1},{25,9},{2,18},{10... | collective-permute-start | bytes 1572872 | tf_op jit(solution)/shard_map/ppermute | solution.py:148
